TPU v7x, 128 devices: a whole 4x4x4 slice. The times are simulated.
128 devices in a mesh: dp: 16 (over y, x), seq: 8 (over z, core).
Axes of the slice: x: 4, y: 4, z: 4, core: 2. Of those that a mesh axis runs over, the one named last changes fastest.
Arguments:
- queries: bfloat16 [32768, 8192], P(('dp', 'seq')), may hold values from -60 to 60
- keys: bfloat16 [32768, 1024], P(('dp', 'seq')), may hold values from -60 to 60
- values: bfloat16 [32768, 1024], P(('dp', 'seq')), may hold values from -6 to 6
- plan: int32 [32768], P(('dp', 'seq')), may hold values from 0 to 32767, as said below
- segment_ids: int32 [32768], P(('dp', 'seq')), may hold values from 0 to 255, as said below
Outputs:
- attended: bfloat16 [32768, 8192], P(('dp', 'seq'))
Inputs may be any that keep to these rules, and one draw needn't show every extreme that they name: `plan`: A permutation of the owner rows. The rows of one device go exactly 2 to each device (owner rows d * 256 to (d + 1) * 256 - 1 belong to device d), in random order among the device's rows. `segment_ids`: documents are runs of equal ids that never fall; every length is a multiple of 128; no document crosses a boundary of the aligned blocks of 2048 owner rows; one document fills a whole block.
All inputs are finite; a program needn't handle non-finite values.
Results may differ from a plain program's by a relative error of at most 0.0053.
Values may be sent and summed in bfloat16 or wider, within the bound.
No kernel may reach another device: no remote copies, remote signals or barrier semaphores. Data moves between devices by JAX's collectives and lax.ppermute only.
A program may use at most 128 MiB of HBM per device.

v0:
```python
import jax
import jax.numpy as jnp
from jax import lax
from jax.sharding import PartitionSpec as P

H = 64
KVH = 8
HD = 128


theta_base = 500000.0
tile_rows = 512


def doc_positions(segment_ids):
    places = jnp.arange(segment_ids.shape[0], dtype=jnp.int32)
    starts = jnp.concatenate([jnp.ones((1,), jnp.bool_), segment_ids[1:] != segment_ids[:-1]])
    first = lax.cummax(jnp.where(starts, places, jnp.zeros_like(places)), axis=0)
    return (places - first, first)


def rotate(source, positions):
    width = source.shape[-1]
    half = width // 2
    freqs = theta_base ** (-2.0 * jnp.arange(half, dtype=jnp.float32) / width)
    angles = positions.astype(jnp.float32)[:, None] * freqs[None, :]
    cosine = jnp.cos(angles)[:, None, :]
    sine = jnp.sin(angles)[:, None, :]
    floats = source.astype(jnp.float32)
    lower = floats[..., :half]
    upper = floats[..., half:]
    turned = jnp.concatenate(
        [lower * cosine - upper * sine, upper * cosine + lower * sine], axis=-1
    )
    return turned.astype(jnp.bfloat16)


def attend_all(group_q, group_k, group_v, group_ids):
    total = group_q.shape[0]
    scale = group_q.shape[-1] ** (-0.5)
    key_rows = jnp.arange(total, dtype=jnp.int32)

    def one_block(number):
        start = number * tile_rows
        block = lax.dynamic_slice_in_dim(group_q, start, tile_rows, 0)
        block_ids = lax.dynamic_slice_in_dim(group_ids, start, tile_rows, 0)
        scores = (
            jnp.einsum("qkgd,tkd->kgqt", block, group_k, preferred_element_type=jnp.float32) * scale
        )
        query_rows = start + jnp.arange(tile_rows, dtype=jnp.int32)
        allowed = (key_rows[None, :] <= query_rows[:, None]) & (
            group_ids[None, :] == block_ids[:, None]
        )
        scores = jnp.where(allowed, scores, -jnp.inf)
        peak = jnp.max(scores, axis=-1, keepdims=True)
        weights = jnp.exp(scores - peak)
        totals = jnp.sum(weights, axis=-1)
        mixed = jnp.einsum(
            "kgqt,tkd->kgqd",
            weights.astype(jnp.bfloat16),
            group_v,
            preferred_element_type=jnp.float32,
        )
        result = mixed / totals[..., None]
        return jnp.transpose(result, (2, 0, 1, 3)).astype(jnp.bfloat16)

    outputs = lax.map(one_block, jnp.arange(total // tile_rows, dtype=jnp.int32))
    return outputs.reshape(group_q.shape)


def settle(arrived, rows_here):
    where_rows = arrived[3].reshape(rows_here)
    placement = jnp.argsort(where_rows)
    own_q = arrived[0].reshape(rows_here, -1)[placement]
    own_k = arrived[1].reshape(rows_here, -1)[placement]
    own_v = arrived[2].reshape(rows_here, -1)[placement]
    return (where_rows, own_q, own_k, own_v)


def per_device(queries, keys, values, plan, segment_ids):
    rows_here = queries.shape[0]
    seq_count = lax.axis_size("seq")
    dp_count = lax.axis_size("dp")
    devices = seq_count * dp_count
    share = rows_here // devices
    group_rows = seq_count * rows_here
    kv_local = KVH // seq_count
    per_kv = H // KVH
    group_ids = lax.all_gather(segment_ids, "seq", axis=0, tiled=True)
    positions, first = doc_positions(group_ids)
    targets = plan // rows_here
    order = jnp.argsort(targets, stable=True)
    sorted_q = queries[order]
    sorted_k = keys[order]
    sorted_v = values[order]
    owner_local = (plan % rows_here)[order].reshape(devices, share)
    arrived = (
        lax.all_to_all(
            sorted_q.reshape(devices, share, -1),
            ("dp", "seq"),
            split_axis=0,
            concat_axis=0,
            tiled=True,
        ),
        lax.all_to_all(
            sorted_k.reshape(devices, share, -1),
            ("dp", "seq"),
            split_axis=0,
            concat_axis=0,
            tiled=True,
        ),
        lax.all_to_all(
            sorted_v.reshape(devices, share, -1),
            ("dp", "seq"),
            split_axis=0,
            concat_axis=0,
            tiled=True,
        ),
        lax.all_to_all(owner_local, ("dp", "seq"), split_axis=0, concat_axis=0, tiled=True),
    )
    where_rows, own_q, own_k, own_v = settle(arrived, rows_here)
    part_q = lax.all_to_all(
        own_q.reshape(rows_here, seq_count, kv_local, per_kv * HD),
        "seq",
        split_axis=1,
        concat_axis=0,
        tiled=True,
    )
    part_k = lax.all_to_all(
        own_k.reshape(rows_here, seq_count, kv_local, HD),
        "seq",
        split_axis=1,
        concat_axis=0,
        tiled=True,
    )
    part_v = lax.all_to_all(
        own_v.reshape(rows_here, seq_count, kv_local, HD),
        "seq",
        split_axis=1,
        concat_axis=0,
        tiled=True,
    )
    items = part_k.shape[2]
    attend_part_q = part_q.reshape(group_rows, items, per_kv * HD)
    attend_part_k = part_k.reshape(group_rows, items, HD)
    attend_part_v = part_v.reshape(group_rows, items, HD)
    attend_items = attend_part_k.shape[1]
    rot_q = rotate(attend_part_q.reshape(group_rows, attend_items * per_kv, HD), positions).reshape(
        group_rows, attend_items, per_kv, HD
    )
    rot_k = rotate(attend_part_k, positions)
    result = attend_all(rot_q, rot_k, attend_part_v, group_ids)
    mixed = result.reshape(group_rows, 1, items, per_kv * HD)
    returned = lax.all_to_all(mixed, "seq", split_axis=0, concat_axis=1, tiled=True)
    owner_out = returned.reshape(rows_here, -1)
    leaving = owner_out[where_rows].reshape(devices, share, -1)
    home = lax.all_to_all(leaving, ("dp", "seq"), split_axis=0, concat_axis=0, tiled=True).reshape(
        rows_here, -1
    )
    return jnp.zeros_like(home).at[order].set(home)


def solution(mesh):
    return jax.shard_map(
        per_device,
        mesh=mesh,
        in_specs=(
            P(("dp", "seq"), None),
            P(("dp", "seq"), None),
            P(("dp", "seq"), None),
            P(("dp", "seq")),
            P(("dp", "seq")),
        ),
        out_specs=P(("dp", "seq"), None),
        check_vma=False,
    )
```

profile of v0, /device:TPU:1, one launch (start us, length us, event | category | flops | bytes accessed | tf_op | source)
XLA Modules:
  0.0 682.4 jit_solution(6127387024564157462)
XLA Ops:
  6.7 11.5 %all-to-all-start.1 = ((s32[128,1,2]{2,1,0:T(1,128)}), s32[128,1,2]{2,1,0:T(1,128)S(1)}, u32[]{:S(2)}, u32[]{:S(2)}) async-start(s32[128,1,2]{2,1,0:T(1,128)} %bitcast.2), calls=%async_computation.1 | async-start | bytes 131072 | tf_op jit(solution)/shard_map/all_to_all | solution.py:119
  34.4 11.5 %all-to-all-done.5 = bf16[128,2,1024]{2,1,0:T(2,128)(2,1)S(1)} async-done(((bf16[128,2,1024]{2,1,0:T(2,128)(2,1)}), bf16[128,2,1024]{2,1,0:T(2,128)(2,1)S(1)}, u32[]{:S(2)}, u32[]{:S(2)}) %all-to-all-start.5) | async-done | bytes 524320 | tf_op jit(solution)/shard_map/all_to_all | solution.py:112
  50.8 11.7 %gather_fusion = bf16[256,8192]{1,0:T(8,128)(2,1)} fusion(bf16[256,8192]{1,0:T(8,128)(2,1)} %param.7, s32[1024]{0:T(1024)S(1)} %pad_clamp_fusion.2), kind=kCustom, calls=%fused_computation | custom fusion | bytes 8389632 | tf_op jit(solution)/shard_map/gather | solution.py:93
  62.5 7.6 %reshape.327 = bf16[128,2,8192]{2,1,0:T(2,128)(2,1)} reshape(bf16[256,8192]{1,0:T(8,128)(2,1)} %gather_fusion) | data formatting | bytes 8388608 | tf_op jit(solution)/shard_map/reshape | solution.py:99
  70.2 10.4 %all-to-all-start = ((bf16[128,2,8192]{2,1,0:T(2,128)(2,1)}), bf16[128,2,8192]{2,1,0:T(2,128)(2,1)}, u32[]{:S(2)}, u32[]{:S(2)}) async-start(bf16[128,2,8192]{2,1,0:T(2,128)(2,1)} %reshape.327), calls=%async_computation | async-start | bytes 8388608 | tf_op jit(solution)/shard_map/all_to_all | solution.py:98
  87.6 45.5 %all-to-all-done = bf16[128,2,8192]{2,1,0:T(2,128)(2,1)} async-done(((bf16[128,2,8192]{2,1,0:T(2,128)(2,1)}), bf16[128,2,8192]{2,1,0:T(2,128)(2,1)}, u32[]{:S(2)}, u32[]{:S(2)}) %all-to-all-start) | async-done | bytes 4194336 | tf_op jit(solution)/shard_map/all_to_all | solution.py:98
  137.6 7.4 %reshape.328 = bf16[256,8192]{1,0:T(8,128)(2,1)} reshape(bf16[128,2,8192]{2,1,0:T(2,128)(2,1)} %all-to-all-done) | data formatting | bytes 8388608 | tf_op jit(solution)/shard_map/reshape | solution.py:74
  144.9 11.6 %gather_fusion.2 = bf16[256,8192]{1,0:T(8,128)(2,1)} fusion(bf16[256,8192]{1,0:T(8,128)(2,1)} %reshape.328, s32[1024]{0:T(1024)S(1)} %pad_clamp_fusion.1), kind=kCustom, calls=%fused_computation.2 | custom fusion | bytes 8389632 | tf_op jit(solution)/shard_map/gather | solution.py:74
  172.7 52.4 %all-gather = s32[8,1,256]{2,1,0:T(1,128)S(1)} all-gather(s32[1,1,256]{2,1,0:T(1,128)S(1)} %bitcast.141), channel_id=1, replica_groups=mesh['dp'=16,'seq'=8] {'seq'}, dimensions={0}, use_global_device_ids=true | all-gather | bytes 9216 | tf_op jit(solution)/shard_map/all_gather | solution.py:89
  262.7 195.5 %while.11 = (s32[]{:T(128)}, bf16[4,512,1,8,128]{4,3,1,0,2:T(8,128)(2,1)}, s32[4]{0:T(128)S(1)}, s32[2048]{0:T(1024)S(1)}, bf16[2048,1,8,128]{3,2,0,1:T(8,128)(2...) while((s32[]{:T(128)}, ...), condition=%wide.region_7.8_spmd.clone, body=%wide.region_4.7_spmd.clone.sunk | while | flops 4391428608 | bytes 112298176 | solution.py:67
  266.6 13.7 %fusion.41 = (f32[8,512]{1,0:T(8,128)S(1)}, f32[512,8,2048]{2,0,1:T(8,128)}) fusion(pred[512,2048]{1,0:T(8,128)(4,1)S(1)} %fusion.40, bf16[2048,1,128]{2,0,1:T(8,128)(2,1)S(1)} %get-tuple-element.189, bf16[512,1,8,128]{3,2,0,1:T(8,128)(2,1)S(1)} %constant_dynamic-slice_fusion.2), kind=kOutput, calls=%fused_computation.14.clone.1 | convolution fusion | flops 2172645376 | bytes 36192256 | tf_op jit(solution)/shard_map/while/body/eval_jaxpr/qkgd,tkd->kgqt/dot_general | solution.py:48
  280.3 15.0 %fusion.42 = f32[8,512]{1,0:T(8,128)S(1)} fusion(f32[512,8,2048]{2,0,1:T(8,128)} %get-tuple-element.160, f32[8,512]{1,0:T(8,128)S(1)} %get-tuple-element.161, pred[512,2048]{1,0:T(8,128)(4,1)S(1)} %fusion.40), kind=kLoop, calls=%fused_computation.12.clone.1 | loop fusion | flops 33550336 | bytes 34635776 | tf_op jit(solution)/shard_map/while/body/eval_jaxpr/reduce_sum | solution.py:57
  295.3 14.7 %fusion.43 = bf16[1,512,1,8,128]{4,1,3,2,0:T(8,128)(2,1)S(1)} fusion(f32[8,512]{1,0:T(8,128)S(1)} %fusion.42, f32[512,8,2048]{2,0,1:T(8,128)} %get-tuple-element.160, f32[8,512]{1,0:T(8,128)S(1)} %get-tuple-element.161, pred[512,2048]{1,0:T(8,128)(4,1)S(1)} %fusion.40, bf16[2048,1,128]{2,0,1:T(8,128)(2,1)S(1)} %get-tuple-element.190), kind=kOutput, calls=%fused_computation.24.clone.1 | convolution fusion | flops 2182086656 | bytes 36208640 | tf_op jit(solution)/shard_map/while/body/eval_jaxpr/kgqt,tkd->kgqd/dot_general | solution.py:58
  315.4 13.7 %fusion.41 = (f32[8,512]{1,0:T(8,128)S(1)}, f32[512,8,2048]{2,0,1:T(8,128)}) fusion(pred[512,2048]{1,0:T(8,128)(4,1)S(1)} %fusion.40, bf16[2048,1,128]{2,0,1:T(8,128)(2,1)S(1)} %get-tuple-element.189, bf16[512,1,8,128]{3,2,0,1:T(8,128)(2,1)S(1)} %constant_dynamic-slice_fusion.2), kind=kOutput, calls=%fused_computation.14.clone.1 | convolution fusion | flops 2172645376 | bytes 36192256 | tf_op jit(solution)/shard_map/while/body/eval_jaxpr/qkgd,tkd->kgqt/dot_general | solution.py:48
  329.1 15.0 %fusion.42 = f32[8,512]{1,0:T(8,128)S(1)} fusion(f32[512,8,2048]{2,0,1:T(8,128)} %get-tuple-element.160, f32[8,512]{1,0:T(8,128)S(1)} %get-tuple-element.161, pred[512,2048]{1,0:T(8,128)(4,1)S(1)} %fusion.40), kind=kLoop, calls=%fused_computation.12.clone.1 | loop fusion | flops 33550336 | bytes 34635776 | tf_op jit(solution)/shard_map/while/body/eval_jaxpr/reduce_sum | solution.py:57
  344.2 14.6 %fusion.43 = bf16[1,512,1,8,128]{4,1,3,2,0:T(8,128)(2,1)S(1)} fusion(f32[8,512]{1,0:T(8,128)S(1)} %fusion.42, f32[512,8,2048]{2,0,1:T(8,128)} %get-tuple-element.160, f32[8,512]{1,0:T(8,128)S(1)} %get-tuple-element.161, pred[512,2048]{1,0:T(8,128)(4,1)S(1)} %fusion.40, bf16[2048,1,128]{2,0,1:T(8,128)(2,1)S(1)} %get-tuple-element.190), kind=kOutput, calls=%fused_computation.24.clone.1 | convolution fusion | flops 2182086656 | bytes 36208640 | tf_op jit(solution)/shard_map/while/body/eval_jaxpr/kgqt,tkd->kgqd/dot_general | solution.py:58
  364.2 13.7 %fusion.41 = (f32[8,512]{1,0:T(8,128)S(1)}, f32[512,8,2048]{2,0,1:T(8,128)}) fusion(pred[512,2048]{1,0:T(8,128)(4,1)S(1)} %fusion.40, bf16[2048,1,128]{2,0,1:T(8,128)(2,1)S(1)} %get-tuple-element.189, bf16[512,1,8,128]{3,2,0,1:T(8,128)(2,1)S(1)} %constant_dynamic-slice_fusion.2), kind=kOutput, calls=%fused_computation.14.clone.1 | convolution fusion | flops 2172645376 | bytes 36192256 | tf_op jit(solution)/shard_map/while/body/eval_jaxpr/qkgd,tkd->kgqt/dot_general | solution.py:48
  377.9 15.0 %fusion.42 = f32[8,512]{1,0:T(8,128)S(1)} fusion(f32[512,8,2048]{2,0,1:T(8,128)} %get-tuple-element.160, f32[8,512]{1,0:T(8,128)S(1)} %get-tuple-element.161, pred[512,2048]{1,0:T(8,128)(4,1)S(1)} %fusion.40), kind=kLoop, calls=%fused_computation.12.clone.1 | loop fusion | flops 33550336 | bytes 34635776 | tf_op jit(solution)/shard_map/while/body/eval_jaxpr/reduce_sum | solution.py:57
  393.0 14.7 %fusion.43 = bf16[1,512,1,8,128]{4,1,3,2,0:T(8,128)(2,1)S(1)} fusion(f32[8,512]{1,0:T(8,128)S(1)} %fusion.42, f32[512,8,2048]{2,0,1:T(8,128)} %get-tuple-element.160, f32[8,512]{1,0:T(8,128)S(1)} %get-tuple-element.161, pred[512,2048]{1,0:T(8,128)(4,1)S(1)} %fusion.40, bf16[2048,1,128]{2,0,1:T(8,128)(2,1)S(1)} %get-tuple-element.190), kind=kOutput, calls=%fused_computation.24.clone.1 | convolution fusion | flops 2182086656 | bytes 36208640 | tf_op jit(solution)/shard_map/while/body/eval_jaxpr/kgqt,tkd->kgqd/dot_general | solution.py:58
  413.1 13.7 %fusion.41 = (f32[8,512]{1,0:T(8,128)S(1)}, f32[512,8,2048]{2,0,1:T(8,128)}) fusion(pred[512,2048]{1,0:T(8,128)(4,1)S(1)} %fusion.40, bf16[2048,1,128]{2,0,1:T(8,128)(2,1)S(1)} %get-tuple-element.189, bf16[512,1,8,128]{3,2,0,1:T(8,128)(2,1)S(1)} %constant_dynamic-slice_fusion.2), kind=kOutput, calls=%fused_computation.14.clone.1 | convolution fusion | flops 2172645376 | bytes 36192256 | tf_op jit(solution)/shard_map/while/body/eval_jaxpr/qkgd,tkd->kgqt/dot_general | solution.py:48
  426.8 15.0 %fusion.42 = f32[8,512]{1,0:T(8,128)S(1)} fusion(f32[512,8,2048]{2,0,1:T(8,128)} %get-tuple-element.160, f32[8,512]{1,0:T(8,128)S(1)} %get-tuple-element.161, pred[512,2048]{1,0:T(8,128)(4,1)S(1)} %fusion.40), kind=kLoop, calls=%fused_computation.12.clone.1 | loop fusion | flops 33550336 | bytes 34635776 | tf_op jit(solution)/shard_map/while/body/eval_jaxpr/reduce_sum | solution.py:57
  441.8 14.7 %fusion.43 = bf16[1,512,1,8,128]{4,1,3,2,0:T(8,128)(2,1)S(1)} fusion(f32[8,512]{1,0:T(8,128)S(1)} %fusion.42, f32[512,8,2048]{2,0,1:T(8,128)} %get-tuple-element.160, f32[8,512]{1,0:T(8,128)S(1)} %get-tuple-element.161, pred[512,2048]{1,0:T(8,128)(4,1)S(1)} %fusion.40, bf16[2048,1,128]{2,0,1:T(8,128)(2,1)S(1)} %get-tuple-element.190), kind=kOutput, calls=%fused_computation.24.clone.1 | convolution fusion | flops 2182086656 | bytes 36208640 | tf_op jit(solution)/shard_map/while/body/eval_jaxpr/kgqt,tkd->kgqd/dot_general | solution.py:58
  458.1 23.8 %reshape_reshape.5 = bf16[2048,1,1,1024]{3,2,1,0:T(2,128)(2,1)} reshape(bf16[4,512,1,8,128]{4,3,1,0,2:T(8,128)(2,1)} %get-tuple-element.51) | data formatting | bytes 8388608 | tf_op jit(solution)/shard_map/reshape;reshape | solution.py:153
  482.4 26.1 %reduce.10 = bf16[2048,1024]{1,0:T(8,128)(2,1)} reduce(bf16[2048,1,1,1024]{3,2,1,0:T(2,128)(2,1)} %reshape_reshape.5, bf16[]{:T(256)} %broadcast.201), dimensions={1,2}, to_apply=%reshape_reshape.5.reduce_sub_computation | reduce | bytes 8388610 | tf_op jit(solution)/shard_map/reshape;reshape | solution.py:153
  508.5 7.8 %reshape.450 = bf16[8,2,131072]{2,1,0:T(2,128)(2,1)} reshape(bf16[2048,1024]{1,0:T(8,128)(2,1)} %reduce.10) | data formatting | bytes 8388608
  521.5 48.7 %all-to-all-done.7 = bf16[8,2,131072]{2,1,0:T(2,128)(2,1)} async-done(((bf16[8,2,131072]{2,1,0:T(2,128)(2,1)}), bf16[8,2,131072]{2,1,0:T(2,128)(2,1)}, u32[]{:S(2)}, u32[]{:S(2)}) %all-to-all-start.7) | async-done | bytes 4194336 | tf_op jit(solution)/shard_map/all_to_all | solution.py:154
  570.2 8.8 %reshape.451 = bf16[2048,1,1,1024]{3,2,1,0:T(2,128)(2,1)} reshape(bf16[8,2,131072]{2,1,0:T(2,128)(2,1)} %all-to-all-done.7) | data formatting | bytes 8388608
  586.6 11.6 %gather_fusion.7 = bf16[256,8192]{1,0:T(8,128)(2,1)} fusion(bf16[256,8192]{1,0:T(8,128)(2,1)} %bitcast.125, s32[1024]{0:T(1024)S(1)} %pad_clamp_fusion), kind=kCustom, calls=%fused_computation.7 | custom fusion | bytes 8389632 | tf_op jit(solution)/shard_map/gather | solution.py:156
  598.2 7.6 %reshape.341 = bf16[128,2,8192]{2,1,0:T(2,128)(2,1)} reshape(bf16[256,8192]{1,0:T(8,128)(2,1)} %gather_fusion.7) | data formatting | bytes 8388608 | tf_op jit(solution)/shard_map/reshape | solution.py:156
  605.8 58.7 %all_to_all.77 = bf16[128,2,8192]{2,1,0:T(2,128)(2,1)} all-to-all(bf16[128,2,8192]{2,1,0:T(2,128)(2,1)} %reshape.341), channel_id=1, replica_groups=mesh['dp'=16,'seq'=8] {'dp','seq'}, dimensions={0} | all-to-all | bytes 8388608 | tf_op jit(solution)/shard_map/all_to_all | solution.py:157
  664.5 7.3 %reshape.415 = bf16[256,8192]{1,0:T(8,128)(2,1)} reshape(bf16[128,2,8192]{2,1,0:T(2,128)(2,1)} %all_to_all.77) | data formatting | bytes 8388608 | tf_op jit(solution)/shard_map/reshape | solution.py:157
  671.8 10.1 %scatter_custom_fusion = bf16[256,8192]{1,0:T(8,128)(2,1)} fusion(s32[256]{0:T(256)} %copy-done.7, bf16[256,8192]{1,0:T(8,128)(2,1)} %reshape.415, bf16[]{:T(256)} %constant.56.clone.1), kind=kCustom, calls=%fused_computation.37 | custom fusion | bytes 4194816 | tf_op jit(solution)/shard_map/scatter | solution.py:160
  (109 shorter events, 124.7 us)
Async XLA Ops:
  0.0 18.2 %copy-start = (bf16[256,1024]{1,0:T(8,128)(2,1)S(1)}, bf16[256,1024]{1,0:T(8,128)(2,1)}, u32[]{:S(2)}) copy-start(bf16[256,1024]{1,0:T(8,128)(2,1)} %param.9) | copy-start | bytes 1572868
  0.0 32.2 %copy-start.2 = (bf16[256,1024]{1,0:T(8,128)(2,1)S(1)}, bf16[256,1024]{1,0:T(8,128)(2,1)}, u32[]{:S(2)}) copy-start(bf16[256,1024]{1,0:T(8,128)(2,1)} %param.8) | copy-start | bytes 1572868
  4.0 2.7 copy-start.7
  6.7 20.9 %all-to-all-start.1 = ((s32[128,1,2]{2,1,0:T(1,128)}), s32[128,1,2]{2,1,0:T(1,128)S(1)}, u32[]{:S(2)}, u32[]{:S(2)}) async-start(s32[128,1,2]{2,1,0:T(1,128)} %bitcast.2), calls=%async_computation.1 | async-start | bytes 131072 | tf_op jit(solution)/shard_map/all_to_all | solution.py:119
  27.6 53.5 %copy-start.5 = (s32[128,1,2]{2,1,0:T(1,128)}, s32[128,1,2]{2,1,0:T(1,128)S(1)}, u32[]{:S(2)}) copy-start(s32[128,1,2]{2,1,0:T(1,128)S(1)} %all-to-all-done.1) | copy-start | bytes 3076
  27.6 18.3 %all-to-all-start.5 = ((bf16[128,2,1024]{2,1,0:T(2,128)(2,1)}), bf16[128,2,1024]{2,1,0:T(2,128)(2,1)S(1)}, u32[]{:S(2)}, u32[]{:S(2)}) async-start(bf16[128,2,1024]{2,1,0:T(2,128)(2,1)} %reshape.335), calls=%async_computation.5 | async-start | bytes 1048576 | tf_op jit(solution)/shard_map/all_to_all | solution.py:112
  45.9 24.3 %all-to-all-start.3 = ((bf16[128,2,1024]{2,1,0:T(2,128)(2,1)}), bf16[128,2,1024]{2,1,0:T(2,128)(2,1)S(1)}, u32[]{:S(2)}, u32[]{:S(2)}) async-start(bf16[128,2,1024]{2,1,0:T(2,128)(2,1)} %reshape.332), calls=%async_computation.3 | async-start | bytes 1048576 | tf_op jit(solution)/shard_map/all_to_all | solution.py:105
  70.2 63.0 %all-to-all-start = ((bf16[128,2,8192]{2,1,0:T(2,128)(2,1)}), bf16[128,2,8192]{2,1,0:T(2,128)(2,1)}, u32[]{:S(2)}, u32[]{:S(2)}) async-start(bf16[128,2,8192]{2,1,0:T(2,128)(2,1)} %reshape.327), calls=%async_computation | async-start | bytes 8388608 | tf_op jit(solution)/shard_map/all_to_all | solution.py:98
  133.1 34.6 %all-to-all-start.4 = ((bf16[256,8,1,128]{3,0,2,1:T(8,128)(2,1)}), bf16[256,8,1,128]{3,0,2,1:T(8,128)(2,1)S(1)}, u32[]{:S(2)}, u32[]{:S(2)}) async-start(bf16[256,8,1,128]{3,0,2,1:T(8,128)(2,1)} %copy.24), calls=%async_computation.4 | async-start | bytes 1048576 | tf_op jit(solution)/shard_map/all_to_all | solution.py:129
  167.8 5.0 copy-start.8
  167.8 69.7 %all-to-all-start.2 = ((bf16[256,8,1,1024]{3,0,2,1:T(8,128)(2,1)}), bf16[256,8,1,1024]{3,0,2,1:T(8,128)(2,1)}, u32[]{:S(2)}, u32[]{:S(2)}) async-start(bf16[256,8,1,1024]{3,0,2,1:T(8,128)(2,1)} %copy.23), calls=%async_computation.2 | async-start | bytes 8388608 | tf_op jit(solution)/shard_map/all_to_all | solution.py:122
  237.5 25.2 %all-to-all-start.6 = ((bf16[256,8,1,128]{3,0,2,1:T(8,128)(2,1)}), bf16[256,8,1,128]{3,0,2,1:T(8,128)(2,1)S(1)}, u32[]{:S(2)}, u32[]{:S(2)}) async-start(bf16[256,8,1,128]{3,0,2,1:T(8,128)(2,1)} %copy.26), calls=%async_computation.6 | async-start | bytes 1048576 | tf_op jit(solution)/shard_map/all_to_all | solution.py:136
  247.6 5.6 copy-start.3
  247.6 5.6 copy-start.4
  516.4 5.0 copy-start.6
  516.4 53.9 %all-to-all-start.7 = ((bf16[8,2,131072]{2,1,0:T(2,128)(2,1)}), bf16[8,2,131072]{2,1,0:T(2,128)(2,1)}, u32[]{:S(2)}, u32[]{:S(2)}) async-start(bf16[8,2,131072]{2,1,0:T(2,128)(2,1)} %reshape.450), calls=%async_computation.7 | async-start | bytes 8388608 | tf_op jit(solution)/shard_map/all_to_all | solution.py:154
  664.5 17.4 %copy-start.1 = (bf16[256,1024]{1,0:T(8,128)(2,1)S(1)}, bf16[256,1024]{1,0:T(8,128)(2,1)}, u32[]{:S(2)}) copy-start(bf16[256,1024]{1,0:T(8,128)(2,1)} %param.9) | copy-start | bytes 1572868
where the time goes:
time: 690 us; the launch traced here: 682 us
  local copies, waits for them, and re-layouts  169 us (24%)
  other arithmetic  123 us (18%)
  waiting for transfers between devices  113 us (16%)
  matrix products  113 us (16%)
  blocking collectives  111 us (16%)
  starting transfers between devices  49.3 us (7%)
    reduce_sum x4, other arithmetic, one_block(): totals = jnp.sum(weights, axis=-1)  60.1 us
    all_to_all x1, blocking collectives, per_device(): lax.all_to_all(leaving, ('dp', 'seq'), split_axis=0, concat_axis=0, tiled...  58.7 us
    dot_general x4, matrix products, one_block(): jnp.einsum('kgqt,tkd->kgqd', weights.astype(jnp.bfloat16), group_v, prefe...  58.6 us
    dot_general x4, matrix products, one_block(): jnp.einsum('qkgd,tkd->kgqt', block, group_k, preferred_element_type=jnp.f...  54.8 us
    all_gather x1, blocking collectives, per_device(): group_ids = lax.all_gather(segment_ids, 'seq', axis=0, tiled=True)  52.4 us
    all_to_all x1, waiting for transfers between devices, per_device(): lax.all_to_all(mixed, 'seq', split_axis=0, concat_axis=1, tiled=True)  48.7 us
    all_to_all x1, waiting for transfers between devices, per_device(): lax.all_to_all(sorted_q.reshape(devices, share, -1), ('dp', 'seq'), split...  45.5 us
    unnamed x29, local copies, waits for them, and re-layouts  37.4 us
  transfers between devices with their start and end apart: 8, of which 4 were waited for; matrix products, arithmetic and copies ran while one was open for 14% of the time, Pallas kernels for 0%

commit v1 on v0

v1 whole, which is shorter than its diff:
```python
import functools

import jax
import jax.numpy as jnp
from jax import lax
from jax.experimental import pallas as pl
from jax.experimental.pallas import tpu as pltpu
from jax.sharding import PartitionSpec as P

H = 64
KVH = 8
HD = 128
ROWS = 256
AXES = ("dp", "seq")
SEQ = 8
GROUPS = 16
DEVICES = SEQ * GROUPS
PER = ROWS // GROUPS
GROUP = SEQ * ROWS
PER_KV = H // KVH
FIRST = 4
BIG = 1e30
theta_base = 500000.0
MIB = 1024 * 1024

f32 = jnp.float32
bf16 = jnp.bfloat16


def params(mib):
    return pltpu.CompilerParams(vmem_limit_bytes=mib * MIB)


def dot(a, b):
    return jnp.dot(a, b, preferred_element_type=f32)


def order_kernel(plan_ref, ids_ref, perm_ref, back_ref, note_ref):
    wide = jnp.broadcast_to(plan_ref[...].astype(f32), (ROWS, ROWS))
    tall = wide.T
    rank_row = jnp.sum((tall < wide).astype(f32), axis=0, keepdims=True).astype(jnp.int32)
    rank_col = jnp.sum((wide < tall).astype(f32), axis=1, keepdims=True).astype(jnp.int32)
    down = lax.broadcasted_iota(jnp.int32, (ROWS, ROWS), 0)
    along = lax.broadcasted_iota(jnp.int32, (ROWS, ROWS), 1)
    perm_ref[...] = (rank_row == down).astype(bf16)
    hit = rank_col == along
    back_ref[...] = hit.astype(bf16)
    ordered = jnp.sum(jnp.where(hit, tall, 0.0), axis=0, keepdims=True)
    note_ref[:, :ROWS] = ordered.astype(jnp.int32)
    lane = lax.broadcasted_iota(jnp.int32, (1, 128), 1)
    halves = ids_ref[...]
    note_ref[:, ROWS:] = jnp.where(lane < 64, halves[:, :1], halves[:, ROWS - 1 :])


def order_rows(plan, segment_ids):
    square = jax.ShapeDtypeStruct((ROWS, ROWS), bf16)
    return pl.pallas_call(
        order_kernel,
        out_shape=(square, square, jax.ShapeDtypeStruct((1, ROWS + 128), jnp.int32)),
        name="order_rows",
    )(plan.reshape(1, ROWS), segment_ids.reshape(1, ROWS))


def pack_kernel(perm_ref, *refs):
    out_ref = refs[-1]
    perm = perm_ref[...]
    at = 0
    for ref in refs[:-1]:
        width = ref.shape[1]
        moved = dot(perm, ref[...]).astype(bf16)
        out_ref[:, 0, :, at : at + width] = moved.reshape(GROUPS, PER, width)
        at += width


def pack(perm, parts):
    width = sum(w for _, w, _ in parts)
    specs = [pl.BlockSpec((ROWS, w), functools.partial(lambda f, h: (0, f(h)), f)) for _, w, f in parts]
    out = pl.pallas_call(
        pack_kernel,
        grid=(SEQ,),
        in_specs=[pl.BlockSpec((ROWS, ROWS), lambda h: (0, 0))] + specs,
        out_specs=pl.BlockSpec((GROUPS, 1, PER, width), lambda h: (0, h, 0, 0)),
        out_shape=jax.ShapeDtypeStruct((GROUPS, SEQ, PER, width), bf16),
        compiler_params=params(24),
        cost_estimate=pl.CostEstimate(
            flops=2 * ROWS * ROWS * SEQ * width,
            bytes_accessed=4 * ROWS * SEQ * width,
            transcendentals=0,
        ),
        name="pack_rows",
    )(perm, *[a for a, _, _ in parts])
    return out.reshape(DEVICES, PER, width)


def unpack_kernel(back_ref, in_ref, *refs):
    out_ref = refs[-1]
    out_ref[...] = dot(back_ref[...], in_ref[:, 0].reshape(ROWS, -1)).astype(bf16)


def unpack(back, home, place, into):
    width = home.shape[-1]
    aliases = {} if into is None else {2: 0}
    more = [] if into is None else [into]
    return pl.pallas_call(
        unpack_kernel,
        grid=(SEQ,),
        in_specs=[
            pl.BlockSpec((ROWS, ROWS), lambda h: (0, 0)),
            pl.BlockSpec((GROUPS, 1, PER, width), lambda h: (0, h, 0, 0)),
        ]
        + [pl.BlockSpec(memory_space=pl.ANY) for _ in more],
        out_specs=pl.BlockSpec((ROWS, width), lambda h: (0, place(h))),
        out_shape=jax.ShapeDtypeStruct((ROWS, H * HD), bf16),
        input_output_aliases=aliases,
        compiler_params=params(24),
        cost_estimate=pl.CostEstimate(
            flops=2 * ROWS * ROWS * SEQ * width,
            bytes_accessed=4 * ROWS * SEQ * width,
            transcendentals=0,
        ),
        name="unpack_rows",
    )(back, home.reshape(GROUPS, SEQ, PER, width), *more)


def tables(notes):
    group = lax.axis_index("dp")
    rows = lax.dynamic_slice(notes, (0, PER * group), (DEVICES, PER)) - GROUP * group
    units = lax.dynamic_slice(notes, (SEQ * group, ROWS), (SEQ, 128))[:, ::64].reshape(16)
    begin = jnp.sum((units[None, :] < units[:, None]).astype(jnp.int32), axis=1)
    number = jnp.arange(16, dtype=jnp.int32)

    rows = rows.reshape(8, 16, 8, 2)
    by_chunk = jnp.transpose(rows, (0, 2, 1, 3)).reshape(GROUP)
    by_block = jnp.transpose(rows, (2, 0, 1, 3)).reshape(GROUP)

    def begin_of(places):
        return jnp.sum(jnp.where((places >> 7)[:, None] == number[None, :], begin[None, :], 0), axis=1)

    position = (by_chunk - 128 * begin_of(by_chunk)).astype(f32)
    freqs = theta_base ** (-2.0 * jnp.arange(HD // 2, dtype=f32) / HD)
    angles = position[:, None] * freqs[None, :]
    cosine = jnp.cos(angles)
    sine = jnp.sin(angles)
    turn_c = jnp.concatenate([cosine, cosine], axis=1)
    turn_s = jnp.concatenate([-sine, sine], axis=1)

    lanes = jnp.arange(HD, dtype=jnp.int32)
    q_mark = jnp.where(lanes[None, :] < begin_of(by_block)[:, None], -BIG, 0.0).astype(bf16)
    k_mark = ((by_block >> 7)[None, :] == lanes[:, None]).astype(bf16)
    blocks = by_block.reshape(SEQ, ROWS)
    causal = jnp.where(blocks[:, None, :] <= blocks[:, :, None], 0.0, -BIG).astype(bf16)
    return turn_c, turn_s, q_mark, k_mark, causal


def attend_kernel(
    xq_ref, xk_ref, xv_ref, turn_c_ref, turn_s_ref, q_mark_ref, k_mark_ref, causal_ref,
    out_ref, perm_ref, back_ref, kt_ref, vv_ref, qs_ref, os_ref,
):
    factor = (HD ** -0.5) * 1.4426950408889634

    def settle(x_ref, chunk, turn):
        moved = dot(perm_ref[...], x_ref[16 * chunk : 16 * chunk + 16].reshape(ROWS, HD))
        if turn:
            here = slice(chunk * ROWS, chunk * ROWS + ROWS)
            moved = moved * turn_c_ref[here, :] + pltpu.roll(moved, HD // 2, 1) * turn_s_ref[here, :]
        return moved.astype(bf16)

    def spread(target, x_ref, turn):
        for chunk in range(8):
            moved = settle(x_ref, chunk, turn)
            for s in range(SEQ):
                at = s * ROWS + chunk * 32
                target[at : at + 32, :HD] = moved[s * 32 : s * 32 + 32]

    @pl.when(pl.program_id(0) == 0)
    def _():
        down = lax.broadcasted_iota(jnp.int32, (ROWS, ROWS), 0)
        along = lax.broadcasted_iota(jnp.int32, (ROWS, ROWS), 1)

        def source(j):
            return ((j >> 1) & 15) * 16 + 2 * (j >> 5) + (j & 1)

        perm_ref[...] = (source(down) == along).astype(bf16)
        back_ref[...] = (source(along) == down).astype(bf16)
        spread(vv_ref, xk_ref, True)
        for s in range(SEQ):
            here = slice(s * ROWS, s * ROWS + ROWS)
            kt_ref[:HD, here] = vv_ref[here, :HD].astype(f32).T.astype(bf16)
        kt_ref[HD:, :] = k_mark_ref[...]
        spread(vv_ref, xv_ref, False)
        vv_ref[:, HD:] = jnp.ones((GROUP, HD), bf16)
        qs_ref[:, HD:] = q_mark_ref[...]

    spread(qs_ref, xq_ref, True)
    for s in range(SEQ):
        here = slice(s * ROWS, s * ROWS + ROWS)
        diagonal = dot(qs_ref[here, :], kt_ref[:, here]) + causal_ref[here, :].astype(f32)
        peak = jnp.max(diagonal, axis=1, keepdims=True)
        if s > 0:
            before = dot(qs_ref[here, :], kt_ref[:, : s * ROWS])
            peak = jnp.maximum(peak, jnp.max(before, axis=1, keepdims=True))
            weight = jnp.exp2((before - peak) * factor).astype(bf16)
            mixed = dot(weight, vv_ref[: s * ROWS, :])
        weight = jnp.exp2((diagonal - peak) * factor).astype(bf16)
        last = dot(weight, vv_ref[here, :])
        mixed = last if s == 0 else mixed + last
        os_ref[here, :] = (mixed[:, :HD] / mixed[:, HD:]).astype(bf16)
    for chunk in range(8):
        rows = [os_ref[s * ROWS + chunk * 32 : s * ROWS + chunk * 32 + 32, :] for s in range(SEQ)]
        moved = dot(back_ref[...], jnp.concatenate(rows, axis=0)).astype(bf16)
        out_ref[16 * chunk : 16 * chunk + 16] = moved.reshape(16, PER, HD)


def attend(heads, q_from, q_at, kv_from, tabs):
    turn_c, turn_s, q_mark, k_mark, causal = tabs

    def block(at):
        return pl.BlockSpec((DEVICES, PER, HD), at)

    def whole(shape):
        return pl.BlockSpec(shape, lambda h: (0, 0))

    pairs = heads * GROUP * GROUP * 36 // 64
    return pl.pallas_call(
        attend_kernel,
        grid=(heads,),
        in_specs=[
            block(lambda h: (0, 0, q_at + h)),
            block(lambda h: (0, 0, 0)),
            block(lambda h: (0, 0, 1)),
            whole((GROUP, HD)),
            whole((GROUP, HD)),
            whole((GROUP, HD)),
            whole((HD, GROUP)),
            whole((GROUP, ROWS)),
        ],
        out_specs=block(lambda h: (0, 0, h)),
        out_shape=jax.ShapeDtypeStruct((DEVICES, PER, heads * HD), bf16),
        scratch_shapes=[
            pltpu.VMEM((ROWS, ROWS), bf16),
            pltpu.VMEM((ROWS, ROWS), bf16),
            pltpu.VMEM((2 * HD, GROUP), bf16),
            pltpu.VMEM((GROUP, 2 * HD), bf16),
            pltpu.VMEM((GROUP, 2 * HD), bf16),
            pltpu.VMEM((GROUP, HD), bf16),
        ],
        compiler_params=params(40),
        cost_estimate=pl.CostEstimate(
            flops=pairs * 2 * 2 * 256,
            bytes_accessed=heads * GROUP * HD * 4 + GROUP * HD * 16,
            transcendentals=pairs,
        ),
        name="attend",
    )(q_from, kv_from, kv_from, turn_c, turn_s, q_mark, k_mark, causal.reshape(GROUP, ROWS))


def exchange(x):
    return lax.all_to_all(x, AXES, split_axis=0, concat_axis=0, tiled=True)


def per_device(queries, keys, values, plan, segment_ids):
    perm, back, note = order_rows(plan, segment_ids)
    notes = lax.all_gather(note, AXES, axis=0, tiled=True)
    half = FIRST * HD
    send_0 = pack(perm, [(keys, HD, lambda h: h), (values, HD, lambda h: h), (queries, half, lambda h: 2 * h)])
    send_1 = pack(perm, [(queries, half, lambda h: 2 * h + 1)])
    got_0 = exchange(send_0)
    got_1 = exchange(send_1)
    tabs = tables(notes)
    out_0 = attend(FIRST, got_0, 2, got_0, tabs)
    home_0 = exchange(out_0)
    out_1 = attend(FIRST, got_1, 0, got_0, tabs)
    home_1 = exchange(out_1)
    partly = unpack(back, home_0, lambda h: 2 * h, None)
    return unpack(back, home_1, lambda h: 2 * h + 1, partly)


def solution(mesh):
    return jax.shard_map(
        per_device,
        mesh=mesh,
        in_specs=(
            P(AXES, None),
            P(AXES, None),
            P(AXES, None),
            P(AXES),
            P(AXES),
        ),
        out_specs=P(AXES, None),
        check_vma=False,
    )
```

time: 690 us -> 238 us (0.34)
  local copies, waits for them, and re-layouts: 169 us -> 26.9 us
  matrix products: 113 us -> 0 us
  other arithmetic: 123 us -> 10.7 us
  waiting for transfers between devices: 113 us -> 25.8 us
  Pallas kernels: 0 us -> 70 us
  blocking collectives: 111 us -> 66.4 us
  starting transfers between devices: 49.3 us -> 36.6 us
    dot_general x8 -> x0, matrix products: 113 us -> none  [the longest x4 58.6 us: one_block(): jnp.einsum('kgqt,tkd->kgqd', weights.astype(jnp.bfloat16), group_v, prefe...]
    all_to_all x8 -> x4, waiting for transfers between devices: 113 us -> 25.8 us  [exchange(): return lax.all_to_all(x, AXES, split_axis=0, concat_axis=0, tiled=True)]
    pallas_call x0 -> x7, Pallas kernels: none -> 70 us  [the longest x2 49.1 us: attend(): pl.pallas_call(attend_kernel, grid=(heads,), in_specs=[block(lambda h: (0...]
    reduce_sum x4 -> x2, other arithmetic: 60.1 us -> 0.3 us  [the longest x1 0.18 us: tables(): begin = jnp.sum((units[None, :] < units[:, None]).astype(jnp.int32), axis=1)]
    all_to_all x1 -> x0, blocking collectives: 58.7 us -> none  [per_device(): lax.all_to_all(leaving, ('dp', 'seq'), split_axis=0, concat_axis=0, tiled...]
    gather x8 -> x0, local copies, waits for them, and re-layouts: 41.6 us -> none  [the longest x1 11.7 us: per_device(): sorted_q = queries[order]]
    reshape x13 -> x3, local copies, waits for them, and re-layouts: 39 us -> 2.72 us  [the longest x1 1.31 us: tables(): by_chunk = jnp.transpose(rows, (0, 2, 1, 3)).reshape(GROUP)]
    another operation x4 -> x0, other arithmetic: 28.8 us -> none  [the longest x1 26.1 us: per_device(): mixed = result.reshape(group_rows, 1, items, per_kv * HD)]
  transfers between devices with their start and end apart: 8 -> 4, of which waited for: 4 -> 1; matrix products, arithmetic and copies ran while one was open for 14% -> 7% of each run, Pallas kernels for 0% -> 24%
where the time goes in v1:
time: 238 us; the launch traced here: 237 us
  Pallas kernels  70 us (29%)
  blocking collectives  66.4 us (28%)
  starting transfers between devices  36.6 us (15%)
  local copies, waits for them, and re-layouts  26.9 us (11%)
  waiting for transfers between devices  25.8 us (11%)
  other arithmetic  10.7 us (4%)
    all_gather x1, blocking collectives, per_device(): notes = lax.all_gather(note, AXES, axis=0, tiled=True)  66.4 us
    pallas_call x2, Pallas kernels, attend(): pl.pallas_call(attend_kernel, grid=(heads,), in_specs=[block(lambda h: (0...  49.1 us
    all_to_all x4, starting transfers between devices, exchange(): return lax.all_to_all(x, AXES, split_axis=0, concat_axis=0, tiled=True)  36.6 us
    all_to_all x4, waiting for transfers between devices, exchange(): return lax.all_to_all(x, AXES, split_axis=0, concat_axis=0, tiled=True)  25.8 us
    unnamed x47, local copies, waits for them, and re-layouts  20.5 us
    pallas_call x2, Pallas kernels, unpack(): pl.pallas_call(unpack_kernel, grid=(SEQ,), in_specs=[pl.BlockSpec((ROWS,...  10.5 us
    pallas_call x2, Pallas kernels, pack(): pl.pallas_call(pack_kernel, grid=(SEQ,), in_specs=[pl.BlockSpec((ROWS, RO...  8.92 us
    neg x1, other arithmetic, tables(): turn_s = jnp.concatenate([-sine, sine], axis=1)  5.84 us
  transfers between devices with their start and end apart: 4, of which 1 were waited for; matrix products, arithmetic and copies ran while one was open for 7% of the time, Pallas kernels for 24%

profile of v1, /device:TPU:1, one launch (start us, length us, event | category | flops | bytes accessed | tf_op | source)
XLA Modules:
  0.0 236.6 jit_solution(13177531899378876648)
XLA Ops:
  0.0 1.6 order_rows.1
  1.6 2.2 copy-done
  4.7 1.0 copy-done.14
  5.7 1.0 copy-done.15
  6.8 4.7 %pack_rows.3 = bf16[16,8,16,768]{3,2,1,0:T(8,128)(2,1)} custom-call(bf16[256,256]{1,0:T(8,128)(2,1)S(1)} %copy-done.12, bf16[256,1024]{1,0:T(8,128)(2,1)S(1)} %copy-done.14, bf16[256,1024]{1,0:T(8,128)(2,1)S(1)} %copy-done.15, bf16[256,8192]{1,0:T(8,128)(2,1)S(1)} %copy-done), custom_call_target="tpu_custom_call" | custom-call | flops 805306368 | bytes 6291456 | tf_op jit(solution)/shard_map/pack_rows/pallas_call | solution.py:78
  11.5 11.5 %all-to-all-start.1 = ((bf16[128,16,768]{2,1,0:T(8,128)(2,1)}), bf16[128,16,768]{2,1,0:T(8,128)(2,1)S(1)}, u32[]{:S(2)}, u32[]{:S(2)}) async-start(bf16[128,16,768]{2,1,0:T(8,128)(2,1)} %bitcast.3), calls=%async_computation.1 | async-start | bytes 6291456 | tf_op jit(solution)/shard_map/all_to_all | solution.py:258
  23.0 66.4 %all-gather = s32[128,1,384]{2,1,0:T(1,128)S(1)} all-gather(s32[1,1,384]{2,1,0:T(1,128)S(1)} %bitcast.27), channel_id=1, replica_groups=mesh['dp'=16,'seq'=8] {'dp','seq'}, dimensions={0}, use_global_device_ids=true | all-gather | bytes 198144 | tf_op jit(solution)/shard_map/all_gather | solution.py:263
  90.4 1.2 copy.30
  91.8 1.3 copy.29
  93.1 1.3 reshape.72
  94.4 1.3 reshape.73
  96.6 1.2 select_convert_fusion.causal_ref
  97.8 2.2 copy-done.1
  100.0 4.2 %pack_rows.2 = bf16[16,8,16,512]{3,2,1,0:T(8,128)(2,1)} custom-call(bf16[256,256]{1,0:T(8,128)(2,1)S(1)} %copy-done.13, bf16[256,8192]{1,0:T(8,128)(2,1)S(1)} %copy-done.1), custom_call_target="tpu_custom_call" | custom-call | flops 536870912 | bytes 4194304 | tf_op jit(solution)/shard_map/pack_rows/pallas_call | solution.py:78
  104.5 5.8 %fusion.1 = (f32[2048,64]{1,0:T(8,128)}, f32[2048,64]{1,0:T(8,128)}, f32[2048,64]{1,0:T(8,128)}) fusion(f32[64]{0:T(128)S(1)} %multiply_power_fusion, f32[2048]{0:T(1024)S(1)} %subtract_convert_fusion), kind=kLoop, calls=%fused_computation.10 | loop fusion | flops 262144 | bytes 1581312 | tf_op jit(solution)/shard_map/neg | solution.py:145
  110.4 5.1 %all-to-all-start = ((bf16[128,16,512]{2,1,0:T(8,128)(2,1)}), bf16[128,16,512]{2,1,0:T(8,128)(2,1)}, u32[]{:S(2)}, u32[]{:S(2)}) async-start(bf16[128,16,512]{2,1,0:T(8,128)(2,1)} %bitcast.2), calls=%async_computation | async-start | bytes 4194304 | tf_op jit(solution)/shard_map/all_to_all | solution.py:258
  115.5 2.9 %pad_maximum_fusion = (f32[2048,128]{1,0:T(8,128)S(1)}, f32[2048,128]{1,0:T(8,128)S(1)}) fusion(f32[2048,64]{1,0:T(8,128)} %get-tuple-element.15, f32[2048,64]{1,0:T(8,128)} %get-tuple-element.14, f32[2048,64]{1,0:T(8,128)} %get-tuple-element.13), kind=kLoop, calls=%fused_computation.4 | loop fusion | flops 524288 | bytes 3670016 | tf_op jit(solution)/shard_map/concatenate | solution.py:144
  119.4 24.3 %attend.3 = bf16[128,16,512]{2,1,0:T(8,128)(2,1)S(1)} custom-call(bf16[128,16,768]{2,1,0:T(8,128)(2,1)S(1)} %all-to-all-done.1.xk_ref.xv_ref.xq_ref, bf16[128,16,768]{2,1,0:T(8,128)(2,1)S(1)} %all-to-all-done.1.xk_ref.xv_ref.xq_ref, bf16[128,16,768]{2,1,0:T(8,128)(2,1)S(1)} %all-to-all-done.1.xk_ref.xv_ref.xq_ref, ...), custom_call_target="tpu_custom_call" | custom-call | flops 9663676416 | bytes 8388608 | tf_op jit(solution)/shard_map/attend/pallas_call | solution.py:224
  143.7 1.4 copy-done.5
  145.1 1.1 copy-done.8
  147.8 9.8 %all-to-all-start.3 = ((bf16[128,16,512]{2,1,0:T(8,128)(2,1)}), bf16[128,16,512]{2,1,0:T(8,128)(2,1)S(1)}, u32[]{:S(2)}, u32[]{:S(2)}) async-start(bf16[128,16,512]{2,1,0:T(8,128)(2,1)} %copy-done.5), calls=%async_computation.3 | async-start | bytes 4194304 | tf_op jit(solution)/shard_map/all_to_all | solution.py:258
  157.6 1.9 copy-done.3
  159.5 1.2 copy-done.9
  160.7 1.2 copy-done.11
  161.9 1.0 copy-done.17
  163.0 1.0 copy-done.19
  164.0 24.8 %attend.2 = bf16[128,16,512]{2,1,0:T(8,128)(2,1)S(1)} custom-call(bf16[128,16,512]{2,1,0:T(8,128)(2,1)} %all-to-all-done.xq_ref, bf16[128,16,768]{2,1,0:T(8,128)(2,1)S(1)} %copy-done.3, bf16[128,16,768]{2,1,0:T(8,128)(2,1)S(1)} %copy-done.3, f32[2048,128]{1,0:T(8,128)S(1)} %copy-done.7, f32[2048,128]{1,0:T(8,128)S(1)} %copy-done.9, ...), custom_call_target="tpu_custom_call" | custom-call | flops 9663676416 | bytes 8388608 | tf_op jit(solution)/shard_map/attend/pallas_call | solution.py:224
  188.8 1.3 copy-done.4
  190.1 10.2 %all-to-all-start.2 = ((bf16[128,16,512]{2,1,0:T(8,128)(2,1)}), bf16[128,16,512]{2,1,0:T(8,128)(2,1)}, u32[]{:S(2)}, u32[]{:S(2)}) async-start(bf16[128,16,512]{2,1,0:T(8,128)(2,1)} %copy-done.4), calls=%async_computation.2 | async-start | bytes 4194304 | tf_op jit(solution)/shard_map/all_to_all | solution.py:258
  200.4 4.1 %unpack_rows.2.refs_0_ = bf16[256,8192]{1,0:T(8,128)(2,1)} custom-call(bf16[256,256]{1,0:T(8,128)(2,1)S(1)} %copy-done.20, bf16[16,8,16,512]{3,2,1,0:T(8,128)(2,1)S(1)} %bitcast.21), custom_call_target="tpu_custom_call" | custom-call | flops 536870912 | bytes 4194304 | tf_op jit(solution)/shard_map/unpack_rows/pallas_call | solution.py:104
  204.4 25.8 %all-to-all-done.2 = bf16[128,16,512]{2,1,0:T(8,128)(2,1)} async-done(((bf16[128,16,512]{2,1,0:T(8,128)(2,1)}), bf16[128,16,512]{2,1,0:T(8,128)(2,1)}, u32[]{:S(2)}, u32[]{:S(2)}) %all-to-all-start.2) | async-done | bytes 2097184 | tf_op jit(solution)/shard_map/all_to_all | solution.py:258
  230.2 6.4 %unpack_rows.3 = bf16[256,8192]{1,0:T(8,128)(2,1)} custom-call(bf16[256,256]{1,0:T(8,128)(2,1)S(1)} %copy-done.20, bf16[16,8,16,512]{3,2,1,0:T(8,128)(2,1)} %bitcast.10.in_ref, bf16[256,8192]{1,0:T(8,128)(2,1)} %unpack_rows.2.refs_0_), custom_call_target="tpu_custom_call", output_to_operand_aliasing={{}: (2, {})} | custom-call | flops 536870912 | bytes 4194304 | tf_op jit(solution)/shard_map/unpack_rows/pallas_call | solution.py:104
  (54 shorter events, 6.0 us)
Async XLA Ops:
  1.6 2.2 copy-start
  3.8 0.9 copy-start.12
  4.7 1.0 copy-start.14
  5.7 1.0 copy-start.15
  11.5 11.5 %copy-start.22 = (s32[1,384]{1,0:T(1,128)S(1)}, s32[1,384]{1,0:T(1,128)}, u32[]{:S(2)}) copy-start(s32[1,384]{1,0:T(1,128)} %get-tuple-element.10) | copy-start | bytes 4612
  11.5 98.9 %all-to-all-start.1 = ((bf16[128,16,768]{2,1,0:T(8,128)(2,1)}), bf16[128,16,768]{2,1,0:T(8,128)(2,1)S(1)}, u32[]{:S(2)}, u32[]{:S(2)}) async-start(bf16[128,16,768]{2,1,0:T(8,128)(2,1)} %bitcast.3), calls=%async_computation.1 | async-start | bytes 6291456 | tf_op jit(solution)/shard_map/all_to_all | solution.py:258
  23.0 74.8 %copy-start.13 = (bf16[256,256]{1,0:T(8,128)(2,1)S(1)}, bf16[256,256]{1,0:T(8,128)(2,1)}, u32[]{:S(2)}) copy-start(bf16[256,256]{1,0:T(8,128)(2,1)} %get-tuple-element.9.perm_ref) | copy-start | bytes 393220
  89.4 0.7 copy-start.21
  97.8 2.2 copy-start.1
  110.4 8.4 %copy-start.2 = (bf16[128,16,768]{2,1,0:T(8,128)(2,1)}, bf16[128,16,768]{2,1,0:T(8,128)(2,1)S(1)}, u32[]{:S(2)}) copy-start(bf16[128,16,768]{2,1,0:T(8,128)(2,1)S(1)} %all-to-all-done.1.xk_ref.xv_ref.xq_ref) | copy-start | bytes 9437188
  110.4 37.4 %all-to-all-start = ((bf16[128,16,512]{2,1,0:T(8,128)(2,1)}), bf16[128,16,512]{2,1,0:T(8,128)(2,1)}, u32[]{:S(2)}, u32[]{:S(2)}) async-start(bf16[128,16,512]{2,1,0:T(8,128)(2,1)} %bitcast.2), calls=%async_computation | async-start | bytes 4194304 | tf_op jit(solution)/shard_map/all_to_all | solution.py:258
  115.4 4.0 %copy-start.10 = (bf16[2048,256]{1,0:T(8,128)(2,1)S(1)}, bf16[2048,256]{1,0:T(8,128)(2,1)}, u32[]{:S(2)}) copy-start(bf16[2048,256]{1,0:T(8,128)(2,1)} %select_convert_fusion.causal_ref) | copy-start | bytes 3145732
  118.3 1.1 copy-start.6
  143.7 1.4 copy-start.5
  145.1 1.1 copy-start.8
  146.1 0.8 copy-start.16
  147.0 0.8 copy-start.18
  147.8 9.8 %copy-start.7 = (f32[2048,128]{1,0:T(8,128)S(1)}, f32[2048,128]{1,0:T(8,128)}, u32[]{:S(2)}) copy-start(f32[2048,128]{1,0:T(8,128)} %copy-done.6) | copy-start | bytes 3145732
  147.8 42.3 %all-to-all-start.3 = ((bf16[128,16,512]{2,1,0:T(8,128)(2,1)}), bf16[128,16,512]{2,1,0:T(8,128)(2,1)S(1)}, u32[]{:S(2)}, u32[]{:S(2)}) async-start(bf16[128,16,512]{2,1,0:T(8,128)(2,1)} %copy-done.5), calls=%async_computation.3 | async-start | bytes 4194304 | tf_op jit(solution)/shard_map/all_to_all | solution.py:258
  157.6 1.9 copy-start.3
  159.5 1.2 copy-start.9
  160.7 1.2 copy-start.11
  161.9 1.0 copy-start.17
  163.0 1.0 copy-start.19
  188.8 1.3 copy-start.4
  190.1 10.2 %copy-start.20 = (bf16[256,256]{1,0:T(8,128)(2,1)S(1)}, bf16[256,256]{1,0:T(8,128)(2,1)}, u32[]{:S(2)}) copy-start(bf16[256,256]{1,0:T(8,128)(2,1)} %get-tuple-element.8.back_ref) | copy-start | bytes 393220
  190.1 40.1 %all-to-all-start.2 = ((bf16[128,16,512]{2,1,0:T(8,128)(2,1)}), bf16[128,16,512]{2,1,0:T(8,128)(2,1)}, u32[]{:S(2)}, u32[]{:S(2)}) async-start(bf16[128,16,512]{2,1,0:T(8,128)(2,1)} %copy-done.4), calls=%async_computation.2 | async-start | bytes 4194304 | tf_op jit(solution)/shard_map/all_to_all | solution.py:258
